TPU v7x, 256 devices: a whole 4x4x8 slice. The times are simulated.
256 devices in a mesh: loop: 4 (over y_hi, core), inner: 64 (over z, x, y_lo).
Axes of the slice: x: 4, y: 4 (y_hi: 2, y_lo: 2; y = y_hi * 2 + y_lo), z: 8, core: 2. Of those that a mesh axis runs over, the one named last changes fastest.
Arguments:
- snapshots: bfloat16 [65536, 1024], P(('loop', 'inner')), may hold values from -6 to 6
- bins: int32 [65536], replicated, may hold values from 0 to 511, as said below
- pairs: int32 [2048, 2], replicated, may hold values from 0 to 511, as said below
- start_weights: bfloat16 [1024, 32], replicated, may hold values from -0.1875 to 0.1875
Outputs:
- basis: float32 [65536, 96], P(('loop', 'inner'))
- coefficients: float32 [4, 32, 32], replicated
Inputs may be any that keep to these rules, and one draw needn't show every extreme that they name: `bins`: the snapshot in row n has a bin in [r * 8, (r + 1) * 8), where r = (n // 256) mod (64). `pairs`: every row (a, b) has a <= b <= a + 8; every bin is paired with itself.
All inputs are finite; a program needn't handle non-finite values.
Results may differ from a plain program's by a relative error of at most 0.0003.
Values may be sent and summed in bfloat16 or wider, within the bound.
A program may use at most 64 MiB of HBM per device.

v0:
```python
import jax
import jax.numpy as jnp
from jax import lax
from jax.sharding import PartitionSpec as P

STEPS = 2
BINS_COL = 8


def extended(cells, sides, width):
    for axis, dim in sides:
        count = lax.axis_size(axis)
        ends = count - 1
        head = lax.slice_in_dim(cells, 0, width, axis=dim)
        tail = lax.slice_in_dim(cells, cells.shape[dim] - width, cells.shape[dim], axis=dim)
        cells = jnp.concatenate(
            [
                lax.ppermute(tail, axis, [(i, (i + 1) % count) for i in range(ends)]),
                cells,
                lax.ppermute(head, axis, [((i + 1) % count, i) for i in range(ends)]),
            ],
            axis=dim,
        )
    return cells


def matches(values, targets):
    return (values[:, None] == targets[None, :]).astype(jnp.float32)


def local_gram(left, right):
    return jnp.dot(left.T, right, precision=lax.Precision.HIGHEST)


def finish(matrix, gram_total):
    lower_factor = jnp.linalg.cholesky(gram_total)
    result = lax.linalg.triangular_solve(
        lower_factor, matrix, left_side=False, lower=True, transpose_a=True
    )
    return (result, lower_factor.T)


def local(snapshots, bins, pairs, start_weights):
    row_count, features = snapshots.shape
    block_width = start_weights.shape[1]
    n_loop = lax.axis_size("loop")
    n_inner = lax.axis_size("inner")
    column = lax.axis_index("inner")
    group = lax.axis_index("loop")
    bin_grid = jnp.pad(
        bins.reshape(n_loop, n_inner, row_count), ((0, 0), (1, 1), (0, 0)), constant_values=-1
    )
    stacked = lax.all_gather(snapshots[None], "loop", axis=0, tiled=True)
    partner_rows = extended(stacked, (("inner", 1),), row_count)
    tile_rows = partner_rows.reshape(n_loop * 3 * row_count, features)
    tile_bins = lax.dynamic_slice_in_dim(bin_grid, column, 3, 1).reshape(-1)
    my_bins = lax.dynamic_slice_in_dim(bins, (group * n_inner + column) * row_count, row_count)
    bin_base = column * BINS_COL
    my_ids = bin_base + jnp.arange(BINS_COL, dtype=jnp.int32)
    window_ids = bin_base - BINS_COL + jnp.arange(3 * BINS_COL, dtype=jnp.int32)
    left_bins = pairs[:, 0]
    right_bins = pairs[:, 1]
    pair_count = jnp.dot(
        matches(left_bins, my_ids).T,
        matches(right_bins, window_ids),
        precision=lax.Precision.HIGHEST,
    )
    pair_count = pair_count + jnp.dot(
        matches(right_bins, my_ids).T,
        matches(left_bins, window_ids),
        precision=lax.Precision.HIGHEST,
    )
    linked_bins = jnp.where(pair_count > 0.5, 1.0, 0.0).astype(jnp.float32)
    my_hot = matches(my_bins, my_ids)
    row_links = jnp.dot(my_hot, linked_bins)
    mine_wide = snapshots.astype(jnp.float32)
    mine_norms = jnp.sum(mine_wide * mine_wide, axis=1)
    epsilon = features / 3.0
    part_hot = matches(tile_bins, window_ids) * (tile_bins >= 0).astype(jnp.float32)[:, None]
    band_mask = jnp.dot(row_links, part_hot.T)
    part_wide = tile_rows.astype(jnp.float32)
    part_norms = jnp.sum(part_wide * part_wide, axis=1)
    products = lax.dot_general(
        snapshots, tile_rows, (((1,), (1,)), ((), ())), preferred_element_type=jnp.float32
    )
    distance = mine_norms[:, None] + part_norms[None, :] - 2.0 * products
    kept_tiles = [band_mask * jnp.exp(-distance / epsilon)]

    def current_kernel(which):
        return kept_tiles[which]

    degree = jnp.sum(current_kernel(0), axis=1)
    inv_root = lax.rsqrt(degree)
    start_block = jnp.dot(snapshots, start_weights, preferred_element_type=jnp.float32)
    start_total = lax.psum(local_gram(start_block, start_block), ("loop", "inner"))
    current, unused = finish(start_block, start_total)
    basis_blocks = [current]
    coefficients = []
    previous = current
    prev_b = jnp.zeros((block_width, block_width), jnp.float32)
    for lanczos_step in range(STEPS):
        scaled = inv_root[:, None] * current
        vec_stack = lax.all_gather(scaled[None], "loop", axis=0, tiled=True)
        vec_strip = extended(vec_stack, (("inner", 1),), row_count)
        strip = vec_strip.reshape(n_loop * 3 * row_count, block_width)
        total = jnp.dot(current_kernel(0), strip, precision=lax.Precision.HIGHEST)
        image = inv_root[:, None] * total
        projected = lax.psum(local_gram(current, image), ("loop", "inner"))
        image = image - jnp.dot(current, projected, precision=lax.Precision.HIGHEST)
        if lanczos_step > 0:
            image = image - jnp.dot(previous, prev_b.T, precision=lax.Precision.HIGHEST)
        gram_total = lax.psum(local_gram(image, image), ("loop", "inner"))
        following, factor = finish(image, gram_total)
        coefficients.append(projected)
        coefficients.append(factor)
        previous = current
        prev_b = factor
        current = following
        basis_blocks.append(current)
    return (jnp.concatenate(basis_blocks, axis=1), jnp.stack(coefficients))


def solution(mesh):
    in_specs = (P(("loop", "inner"), None), P(), P(), P())
    out_specs = (P(("loop", "inner"), None), P())
    return jax.shard_map(local, mesh=mesh, in_specs=in_specs, out_specs=out_specs, check_vma=False)
```

profile of v0, /device:TPU:1, one launch (start us, length us, event | category | flops | bytes accessed | tf_op | source)
XLA Modules:
  0.0 579.3 jit_solution(10393950573843033094)
XLA Ops:
  11.2 90.2 %psum.35 = f32[32,32]{0,1:T(8,128)S(1)} all-reduce(f32[32,32]{0,1:T(8,128)S(1)} %fusion.50), channel_id=1, replica_groups=mesh['loop'=4,'inner'=64] {'loop','inner'}, use_global_device_ids=true, to_apply=%region_0.1 | all-reduce | flops 1024 | bytes 8192 | tf_op jit(solution)/shard_map/psum | solution.py:95
  102.8 5.3 collective-permute-start
  108.1 2.9 cholesky.59
  112.4 2.4 custom-call.7
  118.8 31.0 %collective-permute-done.1 = bf16[4,256,1024]{2,1,0:T(8,128)(2,1)S(1)} collective-permute-done((bf16[4,256,1024]{2,1,0:T(8,128)(2,1)}, bf16[4,256,1024]{2,1,0:T(8,128)(2,1)S(1)}, u32[]{:S(2)}, u32[]{:S(2)}) %collective-permute-start.1) | collective-permute-done | bytes 2097184 | tf_op jit(solution)/shard_map/ppermute | solution.py:20
  149.8 44.7 %collective-permute-done = bf16[4,256,1024]{2,1,0:T(8,128)(2,1)} collective-permute-done((bf16[4,256,1024]{2,1,0:T(8,128)(2,1)}, bf16[4,256,1024]{2,1,0:T(8,128)(2,1)}, u32[]{:S(2)}, u32[]{:S(2)}) %collective-permute-start) | collective-permute-done | bytes 2097184 | tf_op jit(solution)/shard_map/ppermute | solution.py:18
  194.5 3.6 multiply_reduce_fusion
  198.2 3.5 fusion
  201.7 3.1 fusion.46
  205.0 7.2 %all-gather.1 = f32[1024,32]{0,1:T(8,128)S(1)} all-gather(f32[256,32]{0,1:T(8,128)S(1)} %get-tuple-element.20), channel_id=3, replica_groups=mesh['loop'=4,'inner'=64] {'loop'}, dimensions={0}, use_global_device_ids=true | all-gather | bytes 163840 | tf_op jit(solution)/shard_map/all_gather | solution.py:103
  213.6 4.8 collective-permute-start.2
  220.2 3.2 collective-permute-done.2
  223.6 2.8 convolution_multiply_fusion.3
  226.5 80.3 %psum.36 = f32[32,32]{0,1:T(8,128)S(1)} all-reduce(f32[32,32]{0,1:T(8,128)S(1)} %fusion.51), channel_id=1, replica_groups=mesh['loop'=4,'inner'=64] {'loop','inner'}, use_global_device_ids=true, to_apply=%region_6.9 | all-reduce | flops 1024 | bytes 8192 | tf_op jit(solution)/shard_map/psum | solution.py:108
  307.2 75.5 %psum.37 = f32[32,32]{0,1:T(8,128)S(1)} all-reduce(f32[32,32]{0,1:T(8,128)S(1)} %fusion.52), channel_id=1, replica_groups=mesh['loop'=4,'inner'=64] {'loop','inner'}, use_global_device_ids=true, to_apply=%region_7.10 | all-reduce | flops 1024 | bytes 8192 | tf_op jit(solution)/shard_map/psum | solution.py:112
  382.8 2.9 cholesky.70
  390.3 7.4 %all-gather.2 = f32[1024,32]{0,1:T(8,128)S(1)} all-gather(f32[256,32]{0,1:T(8,128)S(1)} %get-tuple-element.22), channel_id=4, replica_groups=mesh['loop'=4,'inner'=64] {'loop'}, dimensions={0}, use_global_device_ids=true | all-gather | bytes 163840 | tf_op jit(solution)/shard_map/all_gather | solution.py:103
  399.1 4.0 collective-permute-start.4
  404.7 2.6 collective-permute-done.4
  407.5 3.5 convolution_multiply_fusion.2
  411.1 76.5 %psum.38 = f32[32,32]{0,1:T(8,128)S(1)} all-reduce(f32[32,32]{0,1:T(8,128)S(1)} %fusion.53), channel_id=1, replica_groups=mesh['loop'=4,'inner'=64] {'loop','inner'}, use_global_device_ids=true, to_apply=%region_8.11 | all-reduce | flops 1024 | bytes 8192 | tf_op jit(solution)/shard_map/psum | solution.py:108
  488.7 75.3 %psum.39 = f32[32,32]{0,1:T(8,128)S(1)} all-reduce(f32[32,32]{0,1:T(8,128)S(1)} %fusion.54), channel_id=1, replica_groups=mesh['loop'=4,'inner'=64] {'loop','inner'}, use_global_device_ids=true, to_apply=%region_9.12 | all-reduce | flops 1024 | bytes 8192 | tf_op jit(solution)/shard_map/psum | solution.py:112
  564.1 2.9 cholesky.81
  568.4 2.4 custom-call.9
  (70 shorter events, 26.8 us)
Async XLA Ops:
  7.2 2.6 copy-start
  7.2 94.4 %all-gather.5.cloned.1.call-start = ((), (), s32[]{:S(2)}) async-start(), calls=%async_computation | async-start | bytes 2621440 | tf_op jit(solution)/shard_map/all_gather | solution.py:53
  101.5 48.3 %collective-permute-start.1 = (bf16[4,256,1024]{2,1,0:T(8,128)(2,1)}, bf16[4,256,1024]{2,1,0:T(8,128)(2,1)S(1)}, u32[]{:S(2)}, u32[]{:S(2)}) collective-permute-start(bf16[4,256,1024]{2,1,0:T(8,128)(2,1)} %bitcast.93), channel_id=1, source_target_pairs={{1,0},{2,1},{3,2},{4,3},{5,4},{6,5},{7,6},{8,7},{9,8},{10,9},{11,1... | collective-permute-start | bytes 6291464 | tf_op jit(solution)/shard_map/ppermute | solution.py:20
  102.8 91.7 %collective-permute-start = (bf16[4,256,1024]{2,1,0:T(8,128)(2,1)}, bf16[4,256,1024]{2,1,0:T(8,128)(2,1)}, u32[]{:S(2)}, u32[]{:S(2)}) collective-permute-start(bf16[4,256,1024]{2,1,0:T(8,128)(2,1)} %bitcast.94), channel_id=1, source_target_pairs={{0,1},{1,2},{2,3},{3,4},{4,5},{5,6},{6,7},{7,8},{8,9},{9,10},{10,1... | collective-permute-start | bytes 6291464 | tf_op jit(solution)/shard_map/ppermute | solution.py:18
  118.8 79.3 %copy-start.1 = (bf16[256,1024]{1,0:T(8,128)(2,1)S(1)}, bf16[256,1024]{1,0:T(8,128)(2,1)}, u32[]{:S(2)}) copy-start(bf16[256,1024]{1,0:T(8,128)(2,1)} %param.7) | copy-start | bytes 1572868
  204.8 185.5 %copy-start.5 = (f32[256]{0:T(256)}, f32[256]{0:T(256)S(1)}, u32[]{:S(2)}) copy-start(f32[256]{0:T(256)S(1)} %rsqrt.7) | copy-start | bytes 3076
  212.3 7.9 %collective-permute-start.3 = (f32[4,256,32]{1,0,2:T(4,128)S(1)}, f32[4,256,32]{1,0,2:T(4,128)S(1)}, u32[]{:S(2)}, u32[]{:S(2)}) collective-permute-start(f32[4,256,32]{1,0,2:T(4,128)S(1)} %reshape.60), channel_id=1, source_target_pairs={{1,0},{2,1},{3,2},{4,3},{5,4},{6,5},{7,6},{8,7},{9,8},{10,9},{11,1... | collective-permute-start | bytes 393224 | tf_op jit(solution)/shard_map/ppermute | solution.py:20
  213.6 9.8 %collective-permute-start.2 = (f32[4,256,32]{1,0,2:T(4,128)S(1)}, f32[4,256,32]{1,0,2:T(4,128)S(1)}, u32[]{:S(2)}, u32[]{:S(2)}) collective-permute-start(f32[4,256,32]{1,0,2:T(4,128)S(1)} %reshape.60), channel_id=1, source_target_pairs={{0,1},{1,2},{2,3},{3,4},{4,5},{5,6},{6,7},{7,8},{8,9},{9,10},{10,1... | collective-permute-start | bytes 393224 | tf_op jit(solution)/shard_map/ppermute | solution.py:18
  306.9 83.4 %copy-start.2 = (f32[32,32]{0,1:T(8,128)}, f32[32,32]{0,1:T(8,128)S(1)}, u32[]{:S(2)}) copy-start(f32[32,32]{0,1:T(8,128)S(1)} %psum.36) | copy-start | bytes 12292
  397.8 173.9 %copy-start.3 = (f32[32,32]{0,1:T(8,128)S(1)}, f32[32,32]{0,1:T(8,128)}, u32[]{:S(2)}) copy-start(f32[32,32]{0,1:T(8,128)} %copy-done.2) | copy-start | bytes 12292
  397.8 173.9 %copy-start.4 = (f32[1,32,32]{1,2,0:T(8,128)S(1)}, f32[1,32,32]{1,2,0:T(8,128)}, u32[]{:S(2)}) copy-start(f32[1,32,32]{1,2,0:T(8,128)} %get-tuple-element.12) | copy-start | bytes 12292
  397.8 6.8 %collective-permute-start.5 = (f32[4,256,32]{1,0,2:T(4,128)S(1)}, f32[4,256,32]{1,0,2:T(4,128)S(1)}, u32[]{:S(2)}, u32[]{:S(2)}) collective-permute-start(f32[4,256,32]{1,0,2:T(4,128)S(1)} %reshape.61), channel_id=1, source_target_pairs={{1,0},{2,1},{3,2},{4,3},{5,4},{6,5},{7,6},{8,7},{9,8},{10,9},{11,1... | collective-permute-start | bytes 393224 | tf_op jit(solution)/shard_map/ppermute | solution.py:20
  399.1 8.2 %collective-permute-start.4 = (f32[4,256,32]{1,0,2:T(4,128)S(1)}, f32[4,256,32]{1,0,2:T(4,128)S(1)}, u32[]{:S(2)}, u32[]{:S(2)}) collective-permute-start(f32[4,256,32]{1,0,2:T(4,128)S(1)} %reshape.61), channel_id=1, source_target_pairs={{0,1},{1,2},{2,3},{3,4},{4,5},{5,6},{6,7},{7,8},{8,9},{9,10},{10,1... | collective-permute-start | bytes 393224 | tf_op jit(solution)/shard_map/ppermute | solution.py:18
Sparse Core Ops, SparseCore 0:
  9.8 33.8 all-gather.4
where the time goes:
time: 581 us; the launch traced here: 579 us
  blocking collectives  413 us (71%)
  waiting for transfers between devices  85.5 us (15%)
  other arithmetic  26.3 us (5%)
  matrix products  18.7 us (3%)
  starting transfers between devices  17.9 us (3%)
  between operations  14.3 us (2%)
    psum x2, blocking collectives, local(): projected = lax.psum(local_gram(current, image), ('loop', 'inner'))  157 us
    psum x2, blocking collectives, local(): gram_total = lax.psum(local_gram(image, image), ('loop', 'inner'))  151 us
    psum x1, blocking collectives, local(): lax.psum(local_gram(start_block, start_block), ('loop', 'inner'))  90.2 us
    ppermute x3, waiting for transfers between devices, extended(): lax.ppermute(tail, axis, [(i, (i + 1) % count) for i in range(ends)])  50.5 us
    ppermute x3, waiting for transfers between devices, extended(): lax.ppermute(head, axis, [((i + 1) % count, i) for i in range(ends)])  34.4 us
    all_gather x2, blocking collectives, local(): vec_stack = lax.all_gather(scaled[None], 'loop', axis=0, tiled=True)  14.7 us
    ppermute x3, starting transfers between devices, extended(): lax.ppermute(tail, axis, [(i, (i + 1) % count) for i in range(ends)])  14 us
  transfers between devices with their start and end apart: 7, of which 6 were waited for; matrix products, arithmetic and copies ran while one was open for 2% of the time, Pallas kernels for 0%

commit v1 on v0

--- a/solution.py
+++ b/solution.py
@@ -109,7 +109,7 @@
         image = image - jnp.dot(current, projected, precision=lax.Precision.HIGHEST)
         if lanczos_step > 0:
             image = image - jnp.dot(previous, prev_b.T, precision=lax.Precision.HIGHEST)
-        gram_total = lax.psum(local_gram(image, image), ("loop", "inner"))
+        gram_total = lax.psum(lax.psum(local_gram(image, image), "inner"), "loop")
         following, factor = finish(image, gram_total)
         coefficients.append(projected)
         coefficients.append(factor)

time: 581 us -> 1070 us (1.84)
  blocking collectives: 413 us -> 900 us
    psum x2 -> x4, blocking collectives: 151 us -> 636 us  [local(): gram_total = lax.psum(lax.psum(local_gram(image, image), 'inner'), 'loop')]
  transfers between devices with their start and end apart: 7 -> 7, of which waited for: 6 -> 6; matrix products, arithmetic and copies ran while one was open for 2% -> 1% of each run, Pallas kernels for 0% -> 0%
where the time goes in v1:
time: 1070 us
  blocking collectives  900 us (84%)
  waiting for transfers between devices  83.8 us (8%)
  other arithmetic  26.3 us (2%)
  matrix products  18.7 us (2%)
  starting transfers between devices  17.9 us (2%)
  between operations  14.3 us (1%)
    psum x4, blocking collectives, local(): gram_total = lax.psum(lax.psum(local_gram(image, image), 'inner'), 'loop')  636 us
    psum x2, blocking collectives, local(): projected = lax.psum(local_gram(current, image), ('loop', 'inner'))  157 us
    psum x1, blocking collectives, local(): lax.psum(local_gram(start_block, start_block), ('loop', 'inner'))  90.2 us
    ppermute x3, waiting for transfers between devices, extended(): lax.ppermute(tail, axis, [(i, (i + 1) % count) for i in range(ends)])  48.7 us
    ppermute x3, waiting for transfers between devices, extended(): lax.ppermute(head, axis, [((i + 1) % count, i) for i in range(ends)])  34.4 us
  transfers between devices with their start and end apart: 7, of which 6 were waited for; matrix products, arithmetic and copies ran while one was open for 1% of the time, Pallas kernels for 0%

profile of v1, /device:TPU:1, one launch (start us, length us, event | category | flops | bytes accessed | tf_op | source)
XLA Modules:
  0.0 1065.1 jit_solution(4597895202075452865)
XLA Ops:
  11.2 90.2 %psum.49 = f32[32,32]{0,1:T(8,128)S(1)} all-reduce(f32[32,32]{0,1:T(8,128)S(1)} %fusion.50), channel_id=1, replica_groups=mesh['loop'=4,'inner'=64] {'loop','inner'}, use_global_device_ids=true, to_apply=%region_0.1 | all-reduce | flops 1024 | bytes 8192 | tf_op jit(solution)/shard_map/psum | solution.py:95
  102.8 5.3 collective-permute-start
  108.1 2.9 cholesky.59
  112.4 2.4 custom-call.7
  118.8 31.0 %collective-permute-done.1 = bf16[4,256,1024]{2,1,0:T(8,128)(2,1)S(1)} collective-permute-done((bf16[4,256,1024]{2,1,0:T(8,128)(2,1)}, bf16[4,256,1024]{2,1,0:T(8,128)(2,1)S(1)}, u32[]{:S(2)}, u32[]{:S(2)}) %collective-permute-start.1) | collective-permute-done | bytes 2097184 | tf_op jit(solution)/shard_map/ppermute | solution.py:20
  149.8 44.7 %collective-permute-done = bf16[4,256,1024]{2,1,0:T(8,128)(2,1)} collective-permute-done((bf16[4,256,1024]{2,1,0:T(8,128)(2,1)}, bf16[4,256,1024]{2,1,0:T(8,128)(2,1)}, u32[]{:S(2)}, u32[]{:S(2)}) %collective-permute-start) | collective-permute-done | bytes 2097184 | tf_op jit(solution)/shard_map/ppermute | solution.py:18
  194.5 3.6 multiply_reduce_fusion
  198.2 3.5 fusion
  201.7 3.1 fusion.46
  205.0 7.2 all-gather.1
  213.6 4.8 collective-permute-start.2
  220.2 3.2 collective-permute-done.2
  223.6 2.8 convolution_multiply_fusion.3
  226.5 80.3 %psum.50 = f32[32,32]{0,1:T(8,128)S(1)} all-reduce(f32[32,32]{0,1:T(8,128)S(1)} %fusion.51), channel_id=1, replica_groups=mesh['loop'=4,'inner'=64] {'loop','inner'}, use_global_device_ids=true, to_apply=%region_6.9 | all-reduce | flops 1024 | bytes 8192 | tf_op jit(solution)/shard_map/psum | solution.py:108
  307.2 251.4 %psum.51 = f32[32,32]{0,1:T(8,128)S(1)} all-reduce(f32[32,32]{0,1:T(8,128)S(1)} %fusion.52), channel_id=1, replica_groups=mesh['loop'=4,'inner'=64] {'inner'}, use_global_device_ids=true, to_apply=%region_7.10 | all-reduce | flops 1024 | bytes 8192 | tf_op jit(solution)/shard_map/psum | solution.py:112
  558.6 66.7 %psum.52 = f32[32,32]{0,1:T(8,128)S(1)} all-reduce(f32[32,32]{0,1:T(8,128)S(1)} %psum.51), channel_id=1, replica_groups=mesh['loop'=4,'inner'=64] {'loop'}, use_global_device_ids=true, to_apply=%region_8.11 | all-reduce | flops 1024 | bytes 8192 | tf_op jit(solution)/shard_map/psum | solution.py:112
  625.3 2.9 cholesky.70
  632.8 9.5 all-gather.2
  643.7 4.0 collective-permute-start.4
  650.3 3.5 convolution_multiply_fusion.2
  653.9 76.9 %psum.53 = f32[32,32]{0,1:T(8,128)S(1)} all-reduce(f32[32,32]{0,1:T(8,128)S(1)} %fusion.53), channel_id=1, replica_groups=mesh['loop'=4,'inner'=64] {'loop','inner'}, use_global_device_ids=true, to_apply=%region_9.12 | all-reduce | flops 1024 | bytes 8192 | tf_op jit(solution)/shard_map/psum | solution.py:108
  731.9 251.4 %psum.54 = f32[32,32]{0,1:T(8,128)S(1)} all-reduce(f32[32,32]{0,1:T(8,128)S(1)} %fusion.54), channel_id=1, replica_groups=mesh['loop'=4,'inner'=64] {'inner'}, use_global_device_ids=true, to_apply=%region_10.13 | all-reduce | flops 1024 | bytes 8192 | tf_op jit(solution)/shard_map/psum | solution.py:112
  983.3 66.5 %psum.55 = f32[32,32]{0,1:T(8,128)S(1)} all-reduce(f32[32,32]{0,1:T(8,128)S(1)} %psum.54), channel_id=1, replica_groups=mesh['loop'=4,'inner'=64] {'loop'}, use_global_device_ids=true, to_apply=%region_11.14 | all-reduce | flops 1024 | bytes 8192 | tf_op jit(solution)/shard_map/psum | solution.py:112
  1049.9 2.9 cholesky.81
  (72 shorter events, 30.1 us)
Async XLA Ops:
  7.2 2.6 copy-start
  7.2 94.4 %all-gather.5.cloned.1.call-start = ((), (), s32[]{:S(2)}) async-start(), calls=%async_computation | async-start | bytes 2621440 | tf_op jit(solution)/shard_map/all_gather | solution.py:53
  101.5 48.3 %collective-permute-start.1 = (bf16[4,256,1024]{2,1,0:T(8,128)(2,1)}, bf16[4,256,1024]{2,1,0:T(8,128)(2,1)S(1)}, u32[]{:S(2)}, u32[]{:S(2)}) collective-permute-start(bf16[4,256,1024]{2,1,0:T(8,128)(2,1)} %bitcast.93), channel_id=1, source_target_pairs={{1,0},{2,1},{3,2},{4,3},{5,4},{6,5},{7,6},{8,7},{9,8},{10,9},{11,1... | collective-permute-start | bytes 6291464 | tf_op jit(solution)/shard_map/ppermute | solution.py:20
  102.8 91.7 %collective-permute-start = (bf16[4,256,1024]{2,1,0:T(8,128)(2,1)}, bf16[4,256,1024]{2,1,0:T(8,128)(2,1)}, u32[]{:S(2)}, u32[]{:S(2)}) collective-permute-start(bf16[4,256,1024]{2,1,0:T(8,128)(2,1)} %bitcast.94), channel_id=1, source_target_pairs={{0,1},{1,2},{2,3},{3,4},{4,5},{5,6},{6,7},{7,8},{8,9},{9,10},{10,1... | collective-permute-start | bytes 6291464 | tf_op jit(solution)/shard_map/ppermute | solution.py:18
  118.8 79.3 %copy-start.1 = (bf16[256,1024]{1,0:T(8,128)(2,1)S(1)}, bf16[256,1024]{1,0:T(8,128)(2,1)}, u32[]{:S(2)}) copy-start(bf16[256,1024]{1,0:T(8,128)(2,1)} %param.7) | copy-start | bytes 1572868
  204.8 428.0 %copy-start.5 = (f32[256]{0:T(256)}, f32[256]{0:T(256)S(1)}, u32[]{:S(2)}) copy-start(f32[256]{0:T(256)S(1)} %rsqrt.7) | copy-start | bytes 3076
  212.3 7.9 collective-permute-start.3
  213.6 9.8 collective-permute-start.2
  306.9 325.9 %copy-start.2 = (f32[32,32]{0,1:T(8,128)}, f32[32,32]{0,1:T(8,128)S(1)}, u32[]{:S(2)}) copy-start(f32[32,32]{0,1:T(8,128)S(1)} %psum.50) | copy-start | bytes 12292
  642.4 415.1 %copy-start.3 = (f32[32,32]{0,1:T(8,128)S(1)}, f32[32,32]{0,1:T(8,128)}, u32[]{:S(2)}) copy-start(f32[32,32]{0,1:T(8,128)} %copy-done.2) | copy-start | bytes 12292
  642.4 415.1 %copy-start.4 = (f32[1,32,32]{1,2,0:T(8,128)S(1)}, f32[1,32,32]{1,2,0:T(8,128)}, u32[]{:S(2)}) copy-start(f32[1,32,32]{1,2,0:T(8,128)} %get-tuple-element.12) | copy-start | bytes 12292
  642.4 6.8 collective-permute-start.5
  643.7 6.4 collective-permute-start.4
Sparse Core Ops, SparseCore 0:
  9.8 33.8 all-gather.4
